TPU v7x, 32 devices: a whole 2x2x4 slice. The times are simulated.
32 devices in a mesh: turn: 4 (over y, core), line: 8 (over z, x).
Axes of the slice: x: 2, y: 2, z: 4, core: 2. Of those that a mesh axis runs over, the one named last changes fastest.
Arguments:
- turn_regret: float32 [16, 8, 1326], P('turn'), may hold values from -6 to 6
- river_regret: float32 [16, 24, 8, 8, 1326], P('turn', 'line'), may hold values from -6 to 6
- opp_reach: float32 [16, 1326], P('turn'), may hold values from 0.1 to 1
- trav_reach: bfloat16 [16, 8, 1326], P('turn'), may hold values from 0 to 1
- pot: float32 [8, 8], replicated, may hold values from 1 to 8
- blockers: int32 [16, 24, 1326], P('turn', 'line'), may hold values 0 or 1
- ranks: int32 [16, 24, 1326], P('turn', 'line'), may hold values from 0 to 7461
Outputs:
- new_turn_regret: float32 [16, 8, 1326], P('turn')
- new_river_regret: float32 [16, 24, 8, 8, 1326], P('turn', 'line')
- root_value: float32 [1326], replicated
All inputs are finite; a program needn't handle non-finite values. No bound on the sum of `blockers` on one device may be relied on, other than what follows from the above.
Results may differ from a plain program's by a relative error of at most 0.0003.
Values sent between devices are 32-bit elements; how exact they have to be, the bound alone decides.
A program may use at most 64 MiB of HBM per device.

v0:
```python
import math

import jax
import jax.numpy as jnp
import numpy as np
from jax import lax
from jax.sharding import PartitionSpec as P

POS_KEEP = 0.99718
NEG_KEEP = 0.5


def regret_match(regret, reduce_axis):
    positive = jnp.maximum(regret, 0.0)
    positive_sum = jnp.sum(positive, axis=reduce_axis, keepdims=True)
    uniform = 1.0 / regret.shape[reduce_axis]
    safe_sum = jnp.where(positive_sum > 0, positive_sum, 1.0)
    return jnp.where(positive_sum > 0, positive / safe_sum, uniform)


def discount(regret):
    return jnp.where(regret > 0, regret * POS_KEEP, regret * NEG_KEEP)


def card_pairs(card_count):
    card_low, card_high = np.triu_indices(card_count, 1)
    return (jnp.asarray(card_low.astype(np.int32)), jnp.asarray(card_high.astype(np.int32)))


def showdown_matrix(rank_row, card_low, card_high):
    clash = (card_low[:, None] == card_low[None, :]) | (card_low[:, None] == card_high[None, :])
    clash = (
        clash
        | (card_high[:, None] == card_low[None, :])
        | (card_high[:, None] == card_high[None, :])
    )
    verdict = jnp.sign(rank_row[:, None] - rank_row[None, :])
    return jnp.where(clash, 0, verdict).astype(jnp.bfloat16)


def runout(reach_pair, regrets, blocked, rank_row, pot, card_low, card_high):
    hand_count = rank_row.shape[0]
    line_count = pot.shape[0]
    unblocked = blocked.astype(jnp.float32)
    strategy = regret_match(regrets, 1)
    opp_part = reach_pair[0].astype(jnp.float32)
    trav_part = reach_pair[1].astype(jnp.float32)
    weighted = jnp.sum(pot[:, :, None] * strategy, axis=1)
    opp_weight = (opp_part * unblocked * weighted).astype(jnp.bfloat16)
    trav_weight = (trav_part * unblocked).astype(jnp.bfloat16)
    stacked = jnp.concatenate([opp_weight, trav_weight], 0)
    showdown = showdown_matrix(rank_row, card_low, card_high)
    product = jnp.einsum("ch,gh->cg", stacked, showdown, preferred_element_type=jnp.float32)
    trav_value = unblocked * product[:line_count] / hand_count
    opp_gain = unblocked * product[line_count:] / hand_count
    action_value = pot[:, :, None] * opp_gain[:, None, :]
    node_value = jnp.sum(strategy * action_value, axis=1)
    updated = discount(regrets) + action_value - node_value[:, None, :]
    return (updated, jnp.stack([trav_value, node_value]))


def body(turn_regret, river_regret, opp_reach, trav_reach, pot, blockers, ranks):
    hand_count = turn_regret.shape[2]
    card_count = (1 + math.isqrt(1 + 8 * hand_count)) // 2
    card_low, card_high = card_pairs(card_count)
    turn_strategy = regret_match(turn_regret, 1)
    opp_lines = (opp_reach[:, None, :] * turn_strategy).astype(jnp.bfloat16)
    reach_pairs = jnp.stack([opp_lines, trav_reach], 1)
    river_count = river_regret.shape[1] * lax.axis_size("line")
    tree_count = turn_regret.shape[0] * lax.axis_size("turn")

    def per_tree(tree_items):
        reach_pair, tree_regrets, tree_blocked, tree_ranks = tree_items

        def per_river(river_items):
            return runout(
                reach_pair, river_items[0], river_items[1], river_items[2], pot, card_low, card_high
            )

        return lax.map(per_river, (tree_regrets, tree_blocked, tree_ranks))

    new_river_regret, values = lax.map(per_tree, (reach_pairs, river_regret, blockers, ranks))
    partial_sums = jnp.sum(values, axis=1)
    trav_float = trav_reach.astype(jnp.float32)
    value_total, gain_total = lax.psum((partial_sums[:, 0], partial_sums[:, 1]), "line")
    line_gain = gain_total / river_count
    local_root = jnp.sum(trav_float * (value_total / river_count), axis=(0, 1))
    root_value = lax.psum(local_root, "turn") / tree_count
    node_turn = jnp.sum(turn_strategy * line_gain, axis=1)
    new_turn_regret = discount(turn_regret) + line_gain - node_turn[:, None, :]
    return (new_turn_regret, new_river_regret, root_value)


def solution(mesh):
    in_specs = (
        P("turn", None, None),
        P("turn", "line", None, None, None),
        P("turn", None),
        P("turn", None, None),
        P(),
        P("turn", "line", None),
        P("turn", "line", None),
    )
    out_specs = (P("turn", None, None), P("turn", "line", None, None, None), P())
    return jax.shard_map(body, mesh=mesh, in_specs=in_specs, out_specs=out_specs, check_vma=False)
```

profile of v0, /device:TPU:0, one launch (start us, length us, event | category | flops | bytes accessed | tf_op | source)
XLA Modules:
  0.0 183.0 jit_solution(1609642143562612694)
XLA Ops:
  7.2 1.0 maximum_reduce_fusion.1
  8.3 1.0 fusion.19
  10.2 80.5 %while.29 = (s32[]{:T(128)}, f32[4,3,8,8,1326]{4,3,2,1,0:T(8,128)}, f32[4,3,2,8,1326]{4,3,2,1,0:T(8,128)}, f32[4,3,8,8,1326]{4,3,2,1,0:T(8,128)}, s32[4,3,1326]{...) while((s32[]{:T(128)}, f32[4,3,8,8,1326]{4,3,2,1,0:T(8,128)}, ...), condition=%wide.region_7.8_spmd.clone, body=%wide.region_1.7_spmd.sunk.clone.sunk | while | flops 77527248 | bytes 7817446 | solution.py:82
  11.3 1.3 dynamic-slice_bitcast_fusion.4
  12.6 15.9 %while.30 = (s32[]{:T(128)}, f32[3,8,8,1326]{3,2,1,0:T(8,128)S(1)}, f32[3,2,8,1326]{3,2,1,0:T(8,128)S(1)}, f32[3,8,8,1326]{3,2,1,0:T(8,128)S(1)}, f32[8,8]{1,0:T...) while((s32[]{:T(128)}, f32[3,8,8,1326]{3,2,1,0:T(8,128)S(1)}, ...), condition=%wide.region_6.6_spmd.clone, body=%wide.region_2.5_spmd.sunk.clone.sunk | while | flops 77527248 | bytes 2900121 | solution.py:80
  13.1 4.4 %fusion.29 = f32[16,1326]{1,0:T(8,128)S(1)} fusion(s32[1326]{0:T(1024)S(1)} %dynamic-slice_reduce_fusion.2, s32[1326]{0:T(1024)S(1)} %get-tuple-element.393, s32[1326]{0:T(1024)S(1)} %get-tuple-element.394, bf16[8,1326]{1,0:T(8,128)(2,1)S(1)} %get-tuple-element.358, bf16[8,1326]{1,0:T(8,128)(2,1)S(1)} %get-tuple-element.359), kind=kOutput, calls=%fused_computation.1.clone.1 | convolution fusion | flops 75690736 | bytes 143208 | tf_op jit(solution)/shard_map/while/body/eval_jaxpr/while/body/eval_jaxpr/ch,gh->cg/dot_general | solution.py:53
  18.4 4.4 %fusion.29 = f32[16,1326]{1,0:T(8,128)S(1)} fusion(s32[1326]{0:T(1024)S(1)} %dynamic-slice_reduce_fusion.2, s32[1326]{0:T(1024)S(1)} %get-tuple-element.393, s32[1326]{0:T(1024)S(1)} %get-tuple-element.394, bf16[8,1326]{1,0:T(8,128)(2,1)S(1)} %get-tuple-element.358, bf16[8,1326]{1,0:T(8,128)(2,1)S(1)} %get-tuple-element.359), kind=kOutput, calls=%fused_computation.1.clone.1 | convolution fusion | flops 75690736 | bytes 143208 | tf_op jit(solution)/shard_map/while/body/eval_jaxpr/while/body/eval_jaxpr/ch,gh->cg/dot_general | solution.py:53
  23.8 4.4 %fusion.29 = f32[16,1326]{1,0:T(8,128)S(1)} fusion(s32[1326]{0:T(1024)S(1)} %dynamic-slice_reduce_fusion.2, s32[1326]{0:T(1024)S(1)} %get-tuple-element.393, s32[1326]{0:T(1024)S(1)} %get-tuple-element.394, bf16[8,1326]{1,0:T(8,128)(2,1)S(1)} %get-tuple-element.358, bf16[8,1326]{1,0:T(8,128)(2,1)S(1)} %get-tuple-element.359), kind=kOutput, calls=%fused_computation.1.clone.1 | convolution fusion | flops 75690736 | bytes 143208 | tf_op jit(solution)/shard_map/while/body/eval_jaxpr/while/body/eval_jaxpr/ch,gh->cg/dot_general | solution.py:53
  29.3 1.0 bitcast_dynamic-update-slice_fusion.4
  30.4 1.0 constant_dynamic-slice_fusion.3
  31.4 1.3 dynamic-slice_bitcast_fusion.4
  32.8 15.9 %while.30 = (s32[]{:T(128)}, f32[3,8,8,1326]{3,2,1,0:T(8,128)S(1)}, f32[3,2,8,1326]{3,2,1,0:T(8,128)S(1)}, f32[3,8,8,1326]{3,2,1,0:T(8,128)S(1)}, f32[8,8]{1,0:T...) while((s32[]{:T(128)}, f32[3,8,8,1326]{3,2,1,0:T(8,128)S(1)}, ...), condition=%wide.region_6.6_spmd.clone, body=%wide.region_2.5_spmd.sunk.clone.sunk | while | flops 77527248 | bytes 2900121 | solution.py:80
  33.3 4.4 %fusion.29 = f32[16,1326]{1,0:T(8,128)S(1)} fusion(s32[1326]{0:T(1024)S(1)} %dynamic-slice_reduce_fusion.2, s32[1326]{0:T(1024)S(1)} %get-tuple-element.393, s32[1326]{0:T(1024)S(1)} %get-tuple-element.394, bf16[8,1326]{1,0:T(8,128)(2,1)S(1)} %get-tuple-element.358, bf16[8,1326]{1,0:T(8,128)(2,1)S(1)} %get-tuple-element.359), kind=kOutput, calls=%fused_computation.1.clone.1 | convolution fusion | flops 75690736 | bytes 143208 | tf_op jit(solution)/shard_map/while/body/eval_jaxpr/while/body/eval_jaxpr/ch,gh->cg/dot_general | solution.py:53
  38.6 4.4 %fusion.29 = f32[16,1326]{1,0:T(8,128)S(1)} fusion(s32[1326]{0:T(1024)S(1)} %dynamic-slice_reduce_fusion.2, s32[1326]{0:T(1024)S(1)} %get-tuple-element.393, s32[1326]{0:T(1024)S(1)} %get-tuple-element.394, bf16[8,1326]{1,0:T(8,128)(2,1)S(1)} %get-tuple-element.358, bf16[8,1326]{1,0:T(8,128)(2,1)S(1)} %get-tuple-element.359), kind=kOutput, calls=%fused_computation.1.clone.1 | convolution fusion | flops 75690736 | bytes 143208 | tf_op jit(solution)/shard_map/while/body/eval_jaxpr/while/body/eval_jaxpr/ch,gh->cg/dot_general | solution.py:53
  43.9 4.4 %fusion.29 = f32[16,1326]{1,0:T(8,128)S(1)} fusion(s32[1326]{0:T(1024)S(1)} %dynamic-slice_reduce_fusion.2, s32[1326]{0:T(1024)S(1)} %get-tuple-element.393, s32[1326]{0:T(1024)S(1)} %get-tuple-element.394, bf16[8,1326]{1,0:T(8,128)(2,1)S(1)} %get-tuple-element.358, bf16[8,1326]{1,0:T(8,128)(2,1)S(1)} %get-tuple-element.359), kind=kOutput, calls=%fused_computation.1.clone.1 | convolution fusion | flops 75690736 | bytes 143208 | tf_op jit(solution)/shard_map/while/body/eval_jaxpr/while/body/eval_jaxpr/ch,gh->cg/dot_general | solution.py:53
  49.4 1.0 bitcast_dynamic-update-slice_fusion.4
  51.5 1.3 dynamic-slice_bitcast_fusion.4
  52.9 15.9 %while.30 = (s32[]{:T(128)}, f32[3,8,8,1326]{3,2,1,0:T(8,128)S(1)}, f32[3,2,8,1326]{3,2,1,0:T(8,128)S(1)}, f32[3,8,8,1326]{3,2,1,0:T(8,128)S(1)}, f32[8,8]{1,0:T...) while((s32[]{:T(128)}, f32[3,8,8,1326]{3,2,1,0:T(8,128)S(1)}, ...), condition=%wide.region_6.6_spmd.clone, body=%wide.region_2.5_spmd.sunk.clone.sunk | while | flops 77527248 | bytes 2900121 | solution.py:80
  53.4 4.4 %fusion.29 = f32[16,1326]{1,0:T(8,128)S(1)} fusion(s32[1326]{0:T(1024)S(1)} %dynamic-slice_reduce_fusion.2, s32[1326]{0:T(1024)S(1)} %get-tuple-element.393, s32[1326]{0:T(1024)S(1)} %get-tuple-element.394, bf16[8,1326]{1,0:T(8,128)(2,1)S(1)} %get-tuple-element.358, bf16[8,1326]{1,0:T(8,128)(2,1)S(1)} %get-tuple-element.359), kind=kOutput, calls=%fused_computation.1.clone.1 | convolution fusion | flops 75690736 | bytes 143208 | tf_op jit(solution)/shard_map/while/body/eval_jaxpr/while/body/eval_jaxpr/ch,gh->cg/dot_general | solution.py:53
  58.7 4.4 %fusion.29 = f32[16,1326]{1,0:T(8,128)S(1)} fusion(s32[1326]{0:T(1024)S(1)} %dynamic-slice_reduce_fusion.2, s32[1326]{0:T(1024)S(1)} %get-tuple-element.393, s32[1326]{0:T(1024)S(1)} %get-tuple-element.394, bf16[8,1326]{1,0:T(8,128)(2,1)S(1)} %get-tuple-element.358, bf16[8,1326]{1,0:T(8,128)(2,1)S(1)} %get-tuple-element.359), kind=kOutput, calls=%fused_computation.1.clone.1 | convolution fusion | flops 75690736 | bytes 143208 | tf_op jit(solution)/shard_map/while/body/eval_jaxpr/while/body/eval_jaxpr/ch,gh->cg/dot_general | solution.py:53
  64.0 4.4 %fusion.29 = f32[16,1326]{1,0:T(8,128)S(1)} fusion(s32[1326]{0:T(1024)S(1)} %dynamic-slice_reduce_fusion.2, s32[1326]{0:T(1024)S(1)} %get-tuple-element.393, s32[1326]{0:T(1024)S(1)} %get-tuple-element.394, bf16[8,1326]{1,0:T(8,128)(2,1)S(1)} %get-tuple-element.358, bf16[8,1326]{1,0:T(8,128)(2,1)S(1)} %get-tuple-element.359), kind=kOutput, calls=%fused_computation.1.clone.1 | convolution fusion | flops 75690736 | bytes 143208 | tf_op jit(solution)/shard_map/while/body/eval_jaxpr/while/body/eval_jaxpr/ch,gh->cg/dot_general | solution.py:53
  69.5 1.0 bitcast_dynamic-update-slice_fusion.4
  71.6 1.3 dynamic-slice_bitcast_fusion.4
  73.0 15.9 %while.30 = (s32[]{:T(128)}, f32[3,8,8,1326]{3,2,1,0:T(8,128)S(1)}, f32[3,2,8,1326]{3,2,1,0:T(8,128)S(1)}, f32[3,8,8,1326]{3,2,1,0:T(8,128)S(1)}, f32[8,8]{1,0:T...) while((s32[]{:T(128)}, f32[3,8,8,1326]{3,2,1,0:T(8,128)S(1)}, ...), condition=%wide.region_6.6_spmd.clone, body=%wide.region_2.5_spmd.sunk.clone.sunk | while | flops 77527248 | bytes 2900121 | solution.py:80
  73.5 4.4 %fusion.29 = f32[16,1326]{1,0:T(8,128)S(1)} fusion(s32[1326]{0:T(1024)S(1)} %dynamic-slice_reduce_fusion.2, s32[1326]{0:T(1024)S(1)} %get-tuple-element.393, s32[1326]{0:T(1024)S(1)} %get-tuple-element.394, bf16[8,1326]{1,0:T(8,128)(2,1)S(1)} %get-tuple-element.358, bf16[8,1326]{1,0:T(8,128)(2,1)S(1)} %get-tuple-element.359), kind=kOutput, calls=%fused_computation.1.clone.1 | convolution fusion | flops 75690736 | bytes 143208 | tf_op jit(solution)/shard_map/while/body/eval_jaxpr/while/body/eval_jaxpr/ch,gh->cg/dot_general | solution.py:53
  78.8 4.4 %fusion.29 = f32[16,1326]{1,0:T(8,128)S(1)} fusion(s32[1326]{0:T(1024)S(1)} %dynamic-slice_reduce_fusion.2, s32[1326]{0:T(1024)S(1)} %get-tuple-element.393, s32[1326]{0:T(1024)S(1)} %get-tuple-element.394, bf16[8,1326]{1,0:T(8,128)(2,1)S(1)} %get-tuple-element.358, bf16[8,1326]{1,0:T(8,128)(2,1)S(1)} %get-tuple-element.359), kind=kOutput, calls=%fused_computation.1.clone.1 | convolution fusion | flops 75690736 | bytes 143208 | tf_op jit(solution)/shard_map/while/body/eval_jaxpr/while/body/eval_jaxpr/ch,gh->cg/dot_general | solution.py:53
  84.1 4.4 %fusion.29 = f32[16,1326]{1,0:T(8,128)S(1)} fusion(s32[1326]{0:T(1024)S(1)} %dynamic-slice_reduce_fusion.2, s32[1326]{0:T(1024)S(1)} %get-tuple-element.393, s32[1326]{0:T(1024)S(1)} %get-tuple-element.394, bf16[8,1326]{1,0:T(8,128)(2,1)S(1)} %get-tuple-element.358, bf16[8,1326]{1,0:T(8,128)(2,1)S(1)} %get-tuple-element.359), kind=kOutput, calls=%fused_computation.1.clone.1 | convolution fusion | flops 75690736 | bytes 143208 | tf_op jit(solution)/shard_map/while/body/eval_jaxpr/while/body/eval_jaxpr/ch,gh->cg/dot_general | solution.py:53
  89.6 1.0 bitcast_dynamic-update-slice_fusion.4
  90.7 1.4 reduce_sum.64
  92.9 74.1 %all-reduce.3.cloned.1.call-done = (f32[4,8,1326]{2,1,0:T(8,128)}, f32[4,8,1326]{2,1,0:T(8,128)}) async-done(((f32[4,8,1326]{2,1,0:T(8,128)}, f32[4,8,1326]{2,1,0:T(8,128)}), (f32[4,8,1326]{2,1,0:T(8,128)}, f32[4,8,1326]{2,1,0:T(8,128)})) %all-reduce.3.cloned.1.call-update) | async-done | bytes 339472 | tf_op jit(solution)/shard_map/psum | solution.py:85
  167.0 1.8 fusion.17
  169.8 5.8 %psum.23 = f32[1326]{0:T(1024)S(1)} all-reduce(f32[1326]{0:T(1024)S(1)} %multiply_reduce_fusion.2), channel_id=1, replica_groups=mesh['turn'=4,'line'=8] {'turn'}, use_global_device_ids=true, to_apply=%region_13.14 | all-reduce | flops 1326 | bytes 10608 | tf_op jit(solution)/shard_map/psum | solution.py:88
  (205 shorter events, 19.7 us)
Async XLA Ops:
  7.2 159.8 %all-reduce.3.cloned.1.call-start = ((), (), s32[]{:S(2)}) async-start(), calls=%async_computation | async-start | bytes 720896 | tf_op jit(solution)/shard_map/psum | solution.py:85
  8.2 2.0 %copy-start.5 = (pred[4,1326]{1,0:T(4,128)(4,1)}, pred[4,1326]{1,0:T(4,128)(4,1)S(1)}, u32[]{:S(2)}) copy-start(pred[4,1326]{1,0:T(4,128)(4,1)S(1)} %broadcast_compare_fusion.1) | copy-start | bytes 15916
  8.2 2.0 %copy-start.3 = (f32[4,1326]{1,0:T(4,128)}, f32[4,1326]{1,0:T(4,128)S(1)}, u32[]{:S(2)}) copy-start(f32[4,1326]{1,0:T(4,128)S(1)} %broadcast_select_fusion.1) | copy-start | bytes 63652
  10.2 2.4 %copy-start = (f32[8,8]{1,0:T(8,128)S(1)}, f32[8,8]{1,0:T(8,128)}, u32[]{:S(2)}) copy-start(f32[8,8]{1,0:T(8,128)} %get-tuple-element.428) | copy-start | bytes 772 | tf_op jit(solution)/shard_map/while
  10.2 2.4 %copy-start.7 = (s32[1326]{0:T(1024)S(1)}, s32[1326]{0:T(1024)}, u32[]{:S(2)}) copy-start(s32[1326]{0:T(1024)} %get-tuple-element.433) | copy-start | bytes 15916 | tf_op jit(solution)/shard_map/while
  10.3 2.4 %copy-start.8 = (s32[1326]{0:T(1024)S(1)}, s32[1326]{0:T(1024)}, u32[]{:S(2)}) copy-start(s32[1326]{0:T(1024)} %get-tuple-element.432) | copy-start | bytes 15916 | tf_op jit(solution)/shard_map/while
  30.4 2.4 %copy-start = (f32[8,8]{1,0:T(8,128)S(1)}, f32[8,8]{1,0:T(8,128)}, u32[]{:S(2)}) copy-start(f32[8,8]{1,0:T(8,128)} %get-tuple-element.428) | copy-start | bytes 772 | tf_op jit(solution)/shard_map/while
  30.4 2.4 %copy-start.7 = (s32[1326]{0:T(1024)S(1)}, s32[1326]{0:T(1024)}, u32[]{:S(2)}) copy-start(s32[1326]{0:T(1024)} %get-tuple-element.433) | copy-start | bytes 15916 | tf_op jit(solution)/shard_map/while
  30.4 2.4 %copy-start.8 = (s32[1326]{0:T(1024)S(1)}, s32[1326]{0:T(1024)}, u32[]{:S(2)}) copy-start(s32[1326]{0:T(1024)} %get-tuple-element.432) | copy-start | bytes 15916 | tf_op jit(solution)/shard_map/while
  50.5 2.4 %copy-start = (f32[8,8]{1,0:T(8,128)S(1)}, f32[8,8]{1,0:T(8,128)}, u32[]{:S(2)}) copy-start(f32[8,8]{1,0:T(8,128)} %get-tuple-element.428) | copy-start | bytes 772 | tf_op jit(solution)/shard_map/while
  50.5 2.4 %copy-start.7 = (s32[1326]{0:T(1024)S(1)}, s32[1326]{0:T(1024)}, u32[]{:S(2)}) copy-start(s32[1326]{0:T(1024)} %get-tuple-element.433) | copy-start | bytes 15916 | tf_op jit(solution)/shard_map/while
  50.5 2.4 %copy-start.8 = (s32[1326]{0:T(1024)S(1)}, s32[1326]{0:T(1024)}, u32[]{:S(2)}) copy-start(s32[1326]{0:T(1024)} %get-tuple-element.432) | copy-start | bytes 15916 | tf_op jit(solution)/shard_map/while
  70.6 2.4 %copy-start = (f32[8,8]{1,0:T(8,128)S(1)}, f32[8,8]{1,0:T(8,128)}, u32[]{:S(2)}) copy-start(f32[8,8]{1,0:T(8,128)} %get-tuple-element.428) | copy-start | bytes 772 | tf_op jit(solution)/shard_map/while
  70.6 2.4 %copy-start.7 = (s32[1326]{0:T(1024)S(1)}, s32[1326]{0:T(1024)}, u32[]{:S(2)}) copy-start(s32[1326]{0:T(1024)} %get-tuple-element.433) | copy-start | bytes 15916 | tf_op jit(solution)/shard_map/while
  70.6 2.4 %copy-start.8 = (s32[1326]{0:T(1024)S(1)}, s32[1326]{0:T(1024)}, u32[]{:S(2)}) copy-start(s32[1326]{0:T(1024)} %get-tuple-element.432) | copy-start | bytes 15916 | tf_op jit(solution)/shard_map/while
  90.7 76.3 %copy-start.1 = (f32[4,8,1326]{2,1,0:T(8,128)S(1)}, f32[4,8,1326]{2,1,0:T(8,128)}, u32[]{:S(2)}) copy-start(f32[4,8,1326]{2,1,0:T(8,128)} %param.13) | copy-start | bytes 509188
  90.7 76.3 %copy-start.4 = (f32[4,1326]{1,0:T(4,128)S(1)}, f32[4,1326]{1,0:T(4,128)}, u32[]{:S(2)}) copy-start(f32[4,1326]{1,0:T(4,128)} %copy-done.3) | copy-start | bytes 63652
  90.7 76.3 %copy-start.6 = (pred[4,1326]{1,0:T(4,128)(4,1)S(1)}, pred[4,1326]{1,0:T(4,128)(4,1)}, u32[]{:S(2)}) copy-start(pred[4,1326]{1,0:T(4,128)(4,1)} %copy-done.5) | copy-start | bytes 15916
  90.7 78.1 %copy-start.2 = (bf16[4,8,1326]{2,1,0:T(8,128)(2,1)S(1)}, bf16[4,8,1326]{2,1,0:T(8,128)(2,1)}, u32[]{:S(2)}) copy-start(bf16[4,8,1326]{2,1,0:T(8,128)(2,1)} %param.16) | copy-start | bytes 254596
Sparse Core Ops, SparseCore 0:
  93.0 73.9 all-reduce.2
where the time goes:
time: 184 us; the launch traced here: 183 us
  waiting for transfers between devices  74.1 us (40%)
  matrix products  52.4 us (28%)
  other arithmetic  17.7 us (10%)
  local copies, waits for them, and re-layouts  17.5 us (10%)
  between operations  14.1 us (8%)
  blocking collectives  5.77 us (3%)
    psum x1, waiting for transfers between devices, body(): lax.psum((partial_sums[:, 0], partial_sums[:, 1]), 'line')  74.1 us
    dot_general x12, matrix products, runout(): jnp.einsum('ch,gh->cg', stacked, showdown, preferred_element_type=jnp.flo...  52.4 us
    dynamic_update_slice x8, local copies, waits for them, and re-layouts, body(): lax.map(per_tree, (reach_pairs, river_regret, blockers, ranks))  7.09 us
    psum x1, blocking collectives, body(): root_value = lax.psum(local_root, 'turn') / tree_count  5.77 us
    squeeze x8, local copies, waits for them, and re-layouts, body(): lax.map(per_tree, (reach_pairs, river_regret, blockers, ranks))  5.3 us
    dynamic_slice x12, local copies, waits for them, and re-layouts, body(): lax.map(per_tree, (reach_pairs, river_regret, blockers, ranks))  3.97 us
  transfers between devices with their start and end apart: 1, of which 1 were waited for; matrix products, arithmetic and copies ran while one was open for 0% of the time, Pallas kernels for 0%

commit v1 on v0

v1 whole, which is shorter than its diff:
```python
import functools
import math

import jax
import jax.numpy as jnp
import numpy as np
from jax import lax
from jax.experimental import pallas as pl
from jax.experimental.pallas import tpu as pltpu
from jax.sharding import PartitionSpec as P

POS_KEEP = 0.99718
NEG_KEEP = 0.5
LANE = 128


def regret_match(regret, reduce_axis):
    positive = jnp.maximum(regret, 0.0)
    positive_sum = jnp.sum(positive, axis=reduce_axis, keepdims=True)
    uniform = 1.0 / regret.shape[reduce_axis]
    safe_sum = jnp.where(positive_sum > 0, positive_sum, 1.0)
    return jnp.where(positive_sum > 0, positive / safe_sum, uniform)


def discount(regret):
    return jnp.maximum(regret * POS_KEEP, regret * NEG_KEEP)


def incidence(hands, padded):
    cards = (1 + math.isqrt(1 + 8 * hands)) // 2
    low, high = np.triu_indices(cards, 1)
    table = np.zeros((padded, LANE), np.float32)
    table[np.arange(hands), low] = 1.0
    table[np.arange(hands), high] = 1.0
    return table


def runout_kernel(
    hands, rivers,
    pot_smem, inc_ref, inc_t_ref, regret_ref, turn_ref, opp_ref, trav_ref, blk_ref, rank_ref,
    out_ref, node_ref, root_ref,
    upper, lower, potb, stacked, phi, col, wgt, prod, root_acc,
):
    tree, river = pl.program_id(0), pl.program_id(1)
    padded = upper.shape[0]
    lines = pot_smem.shape[0]
    first = jnp.logical_and(tree == 0, river == 0)

    @pl.when(first)
    def _():
        stacked[...] = jnp.zeros_like(stacked)
        phi[...] = jnp.zeros_like(phi)
        root_acc[...] = jnp.zeros_like(root_acc)
        row = lax.broadcasted_iota(jnp.int32, (lines, LANE), 0)
        for l in range(lines):
            plane = jnp.zeros((lines, LANE), jnp.float32)
            for m in range(lines):
                plane = jnp.where(row == m, pot_smem[l, m], plane)
            potb[l] = plane
        for start in range(0, padded, LANE):
            rows = pl.ds(start, LANE)
            shared = jnp.dot(inc_ref[rows, :], inc_t_ref[...], preferred_element_type=jnp.float32)
            free = (1.0 - jnp.minimum(shared, 1.0)).astype(jnp.bfloat16)
            upper[rows, :] = free
            lower[rows, :] = -free

    unblocked = blk_ref[0, pl.ds(river, 1), :].astype(jnp.float32)
    rank = rank_ref[0, pl.ds(river, 1), :]
    value = ((rank & 127) + 128).astype(jnp.float32)
    for bit in range(6):
        value = jnp.where((rank & (128 << bit)) != 0, value * float(2 ** (2**bit)), value)
    phi[:, :hands] = jnp.broadcast_to(value, (8, hands))
    col[...] = jnp.broadcast_to(phi[0:1, :], (LANE, padded)).T.astype(jnp.bfloat16)

    turn_strategy = regret_match(turn_ref[0], 0)
    opp_lines = (opp_ref[pl.ds(tree, 1), :] * turn_strategy).astype(jnp.bfloat16)
    opp_part = opp_lines.astype(jnp.float32) * unblocked
    trav = trav_ref[0].astype(jnp.float32)
    for start in range(0, hands, LANE):
        width = min(LANE, hands - start)
        at = pl.ds(start, width)
        pos = jnp.maximum(regret_ref[0, 0, :, :, at], 0.0)
        total = jnp.sum(pos, axis=1)
        potted = jnp.sum(pos * potb[:, :, :width], axis=1)
        mean_pot = jnp.sum(potb[:, :, :width], axis=1) / lines
        some = total > 0
        wgt[:, at] = jnp.where(some, potted / jnp.where(some, total, 1.0), mean_pot)
    weighted = wgt[:, :hands]
    both = jnp.concatenate([opp_part * weighted, trav * unblocked], axis=0)
    stacked[:, :hands] = both.astype(jnp.bfloat16)

    row_phi = [jnp.broadcast_to(phi[:, pl.ds(j, LANE)], (8, LANE)).astype(jnp.bfloat16)[0:1] for j in range(0, padded, LANE)]
    deep = 256
    for n0 in range(0, padded, deep):
        nw = min(deep, padded - n0)
        acc = jnp.zeros((2 * lines, nw), jnp.float32)
        for k0 in range(0, padded, deep):
            kw = min(deep, padded - k0)
            rows = pl.ds(k0, kw)
            parts = []
            for j in range(n0, n0 + nw, LANE):
                gap = row_phi[j // LANE] - col[rows, :]
                cols = pl.ds(j, LANE)
                parts.append(jnp.maximum(jnp.minimum(gap, upper[rows, cols]), lower[rows, cols]))
            acc = acc + jnp.dot(stacked[:, rows], jnp.concatenate(parts, axis=1), preferred_element_type=jnp.float32)
        prod[:, pl.ds(n0, nw)] = acc

    scaled = unblocked / hands
    root_acc[...] += trav * scaled * prod[:lines, :hands]
    gain = scaled * prod[lines:, :hands]
    node = gain * weighted

    @pl.when(river == 0)
    def _():
        node_ref[0] = node

    @pl.when(river > 0)
    def _():
        node_ref[0] += node

    for l in range(lines):
        for start in range(0, hands, LANE):
            width = min(LANE, hands - start)
            at = slice(start, start + width)
            plane = discount(regret_ref[0, 0, l, :, at]) + potb[l, :, :width] * gain[l : l + 1, at]
            out_ref[0, 0, l, :, at] = plane - node[l : l + 1, at]

    @pl.when(jnp.logical_and(tree == pl.num_programs(0) - 1, river == rivers - 1))
    def _():
        root_ref[...] = jnp.sum(root_acc[...], axis=0, keepdims=True)


def run_local(turn_regret, river_regret, opp_reach, trav_reach, pot, blockers, ranks):
    trees, rivers, lines, _, hands = river_regret.shape
    padded = -(-hands // LANE) * LANE
    table = incidence(hands, padded)
    inc, inc_t = jnp.asarray(table, jnp.bfloat16), jnp.asarray(table.T, jnp.bfloat16)
    bf, f32 = jnp.bfloat16, jnp.float32
    per_tree = lambda s, r: (s, 0, 0)
    whole = lambda s, r: (0, 0)
    return pl.pallas_call(
        functools.partial(runout_kernel, hands, rivers),
        grid=(trees, rivers),
        out_shape=(
            jax.ShapeDtypeStruct(river_regret.shape, f32),
            jax.ShapeDtypeStruct((trees, lines, hands), f32),
            jax.ShapeDtypeStruct((1, hands), f32),
        ),
        in_specs=[
            pl.BlockSpec(memory_space=pltpu.SMEM),
            pl.BlockSpec((padded, LANE), whole),
            pl.BlockSpec((LANE, padded), whole),
            pl.BlockSpec((1, 1, lines, lines, hands), lambda s, r: (s, r, 0, 0, 0)),
            pl.BlockSpec((1, lines, hands), per_tree),
            pl.BlockSpec((trees, hands), whole),
            pl.BlockSpec((1, lines, hands), per_tree),
            pl.BlockSpec((1, rivers, hands), per_tree),
            pl.BlockSpec((1, rivers, hands), per_tree),
        ],
        out_specs=(
            pl.BlockSpec((1, 1, lines, lines, hands), lambda s, r: (s, r, 0, 0, 0)),
            pl.BlockSpec((1, lines, hands), per_tree),
            pl.BlockSpec((1, hands), whole),
        ),
        scratch_shapes=[
            pltpu.VMEM((padded, padded), bf),
            pltpu.VMEM((padded, padded), bf),
            pltpu.VMEM((lines, lines, LANE), f32),
            pltpu.VMEM((2 * lines, padded), bf),
            pltpu.VMEM((8, padded), f32),
            pltpu.VMEM((padded, LANE), bf),
            pltpu.VMEM((lines, padded), f32),
            pltpu.VMEM((2 * lines, padded), f32),
            pltpu.VMEM((lines, hands), f32),
        ],
        compiler_params=pltpu.CompilerParams(vmem_limit_bytes=48 * 2**20),
    )(pot, inc, inc_t, river_regret, turn_regret, opp_reach, trav_reach, blockers, ranks)


def body(turn_regret, river_regret, opp_reach, trav_reach, pot, blockers, ranks):
    river_count = river_regret.shape[1] * lax.axis_size("line")
    tree_count = turn_regret.shape[0] * lax.axis_size("turn")
    new_river_regret, node_sum, root = run_local(
        turn_regret, river_regret, opp_reach, trav_reach, pot, blockers, ranks
    )
    line_gain = lax.psum(node_sum, "line") / river_count
    root_value = lax.psum(root[0], ("turn", "line")) / (tree_count * river_count)
    turn_strategy = regret_match(turn_regret, 1)
    node_turn = jnp.sum(turn_strategy * line_gain, axis=1)
    new_turn_regret = discount(turn_regret) + line_gain - node_turn[:, None, :]
    return (new_turn_regret, new_river_regret, root_value)


def solution(mesh):
    in_specs = (
        P("turn", None, None),
        P("turn", "line", None, None, None),
        P("turn", None),
        P("turn", None, None),
        P(),
        P("turn", "line", None),
        P("turn", "line", None),
    )
    out_specs = (P("turn", None, None), P("turn", "line", None, None, None), P())
    return jax.shard_map(body, mesh=mesh, in_specs=in_specs, out_specs=out_specs, check_vma=False)
```

time: 184 us -> 117 us (0.64)
  matrix products: 52.4 us -> 0 us
  waiting for transfers between devices: 74.1 us -> 30 us
  blocking collectives: 5.77 us -> 42.1 us
  Pallas kernels: 0 us -> 18.6 us
  other arithmetic: 17.7 us -> 2.52 us
  local copies, waits for them, and re-layouts: 17.5 us -> 9.27 us
    dot_general x12 -> x0, matrix products: 52.4 us -> none  [runout(): jnp.einsum('ch,gh->cg', stacked, showdown, preferred_element_type=jnp.flo...]
    psum x1, waiting for transfers between devices: 74.1 us -> 30 us  [body(): line_gain = lax.psum(node_sum, 'line') / river_count]
    psum x1, blocking collectives: 5.77 us -> 42.1 us  [body(): lax.psum(root[0], ('turn', 'line')) / (tree_count * river_count)]
    pallas_call x0 -> x1, Pallas kernels: none -> 18.6 us  [run_local(): pl.pallas_call(functools.partial(runout_kernel, hands, rivers), grid=(tre...]
    unnamed x12 -> x18, local copies, waits for them, and re-layouts: 0.03 us -> 9.27 us
    reduce_sum x26 -> x0, other arithmetic: 7.65 us -> none  [the longest x12 2.75 us: runout(): node_value = jnp.sum(strategy * action_value, axis=1)]
    dynamic_update_slice x8 -> x0, local copies, waits for them, and re-layouts: 7.09 us -> none  [body(): lax.map(per_tree, (reach_pairs, river_regret, blockers, ranks))]
    squeeze x9 -> x0, local copies, waits for them, and re-layouts: 6.05 us -> none  [the longest x8 5.3 us: body(): lax.map(per_tree, (reach_pairs, river_regret, blockers, ranks))]
  transfers between devices with their start and end apart: 1 -> 1, of which waited for: 1 -> 1; matrix products, arithmetic and copies ran while one was open for 0% -> 1% of each run, Pallas kernels for 0% -> 0%
where the time goes in v1:
time: 117 us
  blocking collectives  42.1 us (36%)
  waiting for transfers between devices  30 us (26%)
  Pallas kernels  18.6 us (16%)
  between operations  14.1 us (12%)
  local copies, waits for them, and re-layouts  9.27 us (8%)
  other arithmetic  2.52 us (2%)
    psum x1, blocking collectives, body(): lax.psum(root[0], ('turn', 'line')) / (tree_count * river_count)  42.1 us
    psum x1, waiting for transfers between devices, body(): line_gain = lax.psum(node_sum, 'line') / river_count  30 us
    pallas_call x1, Pallas kernels, run_local(): pl.pallas_call(functools.partial(runout_kernel, hands, rivers), grid=(tre...  18.6 us
    unnamed x18, local copies, waits for them, and re-layouts  9.27 us
  transfers between devices with their start and end apart: 1, of which 1 were waited for; matrix products, arithmetic and copies ran while one was open for 1% of the time, Pallas kernels for 0%

profile of v1, /device:TPU:0, one launch (start us, length us, event | category | flops | bytes accessed | tf_op | source)
XLA Modules:
  0.0 116.6 jit_solution(13372672920945148781)
XLA Ops:
  7.2 0.0 copy-start.2
  7.2 0.0 all-reduce.2.cloned.1.call-start
  7.2 0.9 copy.12.blk_ref
  8.2 0.9 copy.13.rank_ref
  9.1 0.0 copy-start
  9.1 2.2 %copy-done = f32[4,3,8,8,1326]{4,3,2,1,0:T(8,128)S(1)} copy-done((f32[4,3,8,8,1326]{4,3,2,1,0:T(8,128)S(1)}, f32[4,3,8,8,1326]{4,3,2,1,0:T(8,128)}, u32[]{:S(2)}) %copy-start) | copy-done | bytes 4073496
  11.3 0.0 copy-start.1
  11.3 0.9 copy-done.1
  12.2 0.0 copy-start.3
  12.2 1.0 copy-done.3
  13.2 0.0 copy-start.4
  13.2 1.0 copy-done.4
  14.2 0.0 copy-start.5
  14.2 0.9 copy-done.5
  15.1 0.0 copy-start.6
  15.1 0.7 copy-done.6
  15.8 0.0 copy-start.7
  15.8 0.7 copy-done.7
  16.5 18.6 %shard_map.112 = (f32[4,3,8,8,1326]{4,3,2,1,0:T(8,128)}, f32[4,8,1326]{2,1,0:T(8,128)}, f32[1,1326]{1,0:T(1,128)S(1)}) custom-call(f32[8,8]{1,0:T(8,128)S(1)} %copy-done.7, bf16[1408,128]{1,0:T(8,128)(2,1)S(1)} %copy-done.3, bf16[128,1408]{1,0:T(8,128)(2,1)S(1)} %copy-done.4, f32[4,3,8,8,1326]{4,3,2,1,0:T(8,128)S(1)} %copy-done, ...), custom_call_target="tpu_custom_call" | custom-call | tf_op jit(solution)/shard_map/pallas_call | solution.py:141
  35.1 0.0 all-reduce.2.cloned.1.call-update
  35.1 0.0 copy-done.2
  35.1 0.1 maximum_reduce_fusion
  35.2 42.1 %psum.15 = f32[1326]{0:T(1024)S(1)} all-reduce(f32[1326]{0:T(1024)S(1)} %reduce), channel_id=1, replica_groups=mesh['turn'=4,'line'=8] {'turn','line'}, use_global_device_ids=true, to_apply=%region_3.4 | all-reduce | flops 1326 | bytes 10608 | tf_op jit(solution)/shard_map/psum | solution.py:187
  77.3 0.6 broadcast_multiply_fusion
  77.9 30.0 %all-reduce.2.cloned.1.call-done = f32[4,8,1326]{2,1,0:T(8,128)} async-done(((f32[4,8,1326]{2,1,0:T(8,128)}), f32[4,8,1326]{2,1,0:T(8,128)}) %all-reduce.2.cloned.1.call-update) | async-done | bytes 169744 | tf_op jit(solution)/shard_map/psum | solution.py:186
  107.9 1.8 %fusion.1 = f32[4,8,1326]{2,1,0:T(8,128)} fusion(f32[4,8,1326]{2,1,0:T(8,128)S(1)} %copy-done.2, f32[4,8,1326]{2,1,0:T(8,128)} %all-reduce.2.cloned.1.call-done, f32[4,1326]{1,0:T(4,128)S(1)} %broadcast_select_fusion, pred[4,1326]{1,0:T(4,128)(4,1)S(1)} %broadcast_compare_fusion), kind=kOutput, calls=%fused_computation.1 | output fusion | flops 472063 | bytes 535704 | tf_op jit(solution)/shard_map/sub | solution.py:190
  (3 shorter events, 0.0 us)
Async XLA Ops:
  7.2 27.9 %copy-start.2 = (f32[4,8,1326]{2,1,0:T(8,128)S(1)}, f32[4,8,1326]{2,1,0:T(8,128)}, u32[]{:S(2)}) copy-start(f32[4,8,1326]{2,1,0:T(8,128)} %turn_ref.1) | copy-start | bytes 509188
  7.2 100.8 %all-reduce.2.cloned.1.call-start = ((), (), s32[]{:S(2)}) async-start(), calls=%async_computation | async-start | bytes 360448 | tf_op jit(solution)/shard_map/psum | solution.py:186
  9.1 2.2 %copy-start = (f32[4,3,8,8,1326]{4,3,2,1,0:T(8,128)S(1)}, f32[4,3,8,8,1326]{4,3,2,1,0:T(8,128)}, u32[]{:S(2)}) copy-start(f32[4,3,8,8,1326]{4,3,2,1,0:T(8,128)} %regret_ref.1) | copy-start | bytes 12220420
  11.3 0.9 copy-start.1
  12.2 1.0 copy-start.3
  13.2 1.0 copy-start.4
  14.2 0.9 copy-start.5
  15.1 0.7 copy-start.6
  15.8 0.7 copy-start.7
Sparse Core Ops, SparseCore 0:
  35.2 72.6 all-reduce.1

commit v2 on v1

--- a/solution.py
+++ b/solution.py
@@ -37,7 +37,7 @@
 
 def runout_kernel(
     hands, rivers,
-    pot_smem, inc_ref, inc_t_ref, regret_ref, turn_ref, opp_ref, trav_ref, blk_ref, rank_ref,
+    pot_smem, inc_ref, regret_ref, turn_ref, opp_ref, trav_ref, code_ref,
     out_ref, node_ref, root_ref,
     upper, lower, potb, stacked, phi, col, wgt, prod, root_acc,
 ):
@@ -59,13 +59,17 @@
             potb[l] = plane
         for start in range(0, padded, LANE):
             rows = pl.ds(start, LANE)
-            shared = jnp.dot(inc_ref[rows, :], inc_t_ref[...], preferred_element_type=jnp.float32)
+            shared = lax.dot_general(
+                inc_ref[rows, :], inc_ref[...], (((1,), (1,)), ((), ())),
+                preferred_element_type=jnp.float32,
+            )
             free = (1.0 - jnp.minimum(shared, 1.0)).astype(jnp.bfloat16)
             upper[rows, :] = free
             lower[rows, :] = -free
 
-    unblocked = blk_ref[0, pl.ds(river, 1), :].astype(jnp.float32)
-    rank = rank_ref[0, pl.ds(river, 1), :]
+    code = code_ref[0, pl.ds(river, 1), :]
+    unblocked = (code & 1).astype(jnp.float32)
+    rank = code >> 1
     value = ((rank & 127) + 128).astype(jnp.float32)
     for bit in range(6):
         value = jnp.where((rank & (128 << bit)) != 0, value * float(2 ** (2**bit)), value)
@@ -134,7 +138,8 @@
     trees, rivers, lines, _, hands = river_regret.shape
     padded = -(-hands // LANE) * LANE
     table = incidence(hands, padded)
-    inc, inc_t = jnp.asarray(table, jnp.bfloat16), jnp.asarray(table.T, jnp.bfloat16)
+    inc = jnp.asarray(table, jnp.bfloat16)
+    codes = jnp.pad(ranks * 2 + blockers, ((0, 0), (0, -rivers % 8), (0, 0)))
     bf, f32 = jnp.bfloat16, jnp.float32
     per_tree = lambda s, r: (s, 0, 0)
     whole = lambda s, r: (0, 0)
@@ -149,13 +154,11 @@
         in_specs=[
             pl.BlockSpec(memory_space=pltpu.SMEM),
             pl.BlockSpec((padded, LANE), whole),
-            pl.BlockSpec((LANE, padded), whole),
             pl.BlockSpec((1, 1, lines, lines, hands), lambda s, r: (s, r, 0, 0, 0)),
             pl.BlockSpec((1, lines, hands), per_tree),
             pl.BlockSpec((trees, hands), whole),
             pl.BlockSpec((1, lines, hands), per_tree),
-            pl.BlockSpec((1, rivers, hands), per_tree),
-            pl.BlockSpec((1, rivers, hands), per_tree),
+            pl.BlockSpec((1, codes.shape[1], hands), per_tree),
         ],
         out_specs=(
             pl.BlockSpec((1, 1, lines, lines, hands), lambda s, r: (s, r, 0, 0, 0)),
@@ -173,8 +176,140 @@
             pltpu.VMEM((2 * lines, padded), f32),
             pltpu.VMEM((lines, hands), f32),
         ],
-        compiler_params=pltpu.CompilerParams(vmem_limit_bytes=48 * 2**20),
-    )(pot, inc, inc_t, river_regret, turn_regret, opp_reach, trav_reach, blockers, ranks)
+        compiler_params=pltpu.CompilerParams(vmem_limit_bytes=60 * 2**20),
+    )(pot, inc, river_regret, turn_regret, opp_reach, trav_reach, codes)
+
+
+def combine_kernel(
+    line_size, turn_size, river_count, tree_count,
+    node_ref, root_ref, turn_ref, out_ref, value_ref,
+    outbox, inbox, total, gather, root_total, root_box, gain,
+    send1, recv1, send2, recv2, send3, recv3,
+):
+    me, mine = lax.axis_index("line"), lax.axis_index("turn")
+    line_peers = [lax.rem(me + i, line_size) for i in range(1, line_size)]
+    turn_peers = [lax.rem(mine + i, turn_size) for i in range(1, turn_size)]
+    mesh_ids = pl.DeviceIdType.MESH
+    barrier = pltpu.get_barrier_semaphore()
+    for peer in line_peers:
+        pl.semaphore_signal(barrier, inc=1, device_id=(mine, peer), device_id_type=mesh_ids)
+    for peer in turn_peers:
+        pl.semaphore_signal(barrier, inc=1, device_id=(peer, me), device_id_type=mesh_ids)
+
+    trees, lines, hands = node_ref.shape
+    rows = trees * lines // line_size
+    tiles = -(-hands // LANE)
+    spans = [(j, min(LANE, hands - j * LANE)) for j in range(tiles)]
+    outbox[...] = jnp.zeros_like(outbox)
+    gain[...] = jnp.zeros_like(gain)
+    for j, width in spans:
+        at = pl.ds(j * LANE, width)
+        for d in range(line_size):
+            tree, line = divmod(d * rows, lines)
+            outbox[d, pl.ds(j * rows, rows), :width] = node_ref[tree, pl.ds(line, rows), at]
+            outbox[d, pl.ds(tiles * rows + j, 1), :width] = root_ref[:, at]
+    pl.semaphore_wait(barrier, line_size + turn_size - 2)
+
+    firsts = []
+    for peer in line_peers:
+        copy = pltpu.make_async_remote_copy(
+            src_ref=outbox.at[peer], dst_ref=inbox.at[me], send_sem=send1.at[peer],
+            recv_sem=recv1.at[me], device_id=(mine, peer), device_id_type=mesh_ids,
+        )
+        copy.start()
+        firsts.append(copy)
+    inbox[me] = outbox[me]
+    for peer in line_peers:
+        pltpu.make_async_remote_copy(
+            src_ref=outbox.at[peer], dst_ref=inbox.at[peer], send_sem=send1.at[peer],
+            recv_sem=recv1.at[peer], device_id=(mine, peer), device_id_type=mesh_ids,
+        ).wait_recv()
+    summed = inbox[0]
+    for d in range(1, line_size):
+        summed = summed + inbox[d]
+    total[...] = summed[: total.shape[0]]
+    root_total[...] = jnp.zeros_like(root_total)
+    root_total[:tiles, :] = summed[tiles * rows : tiles * rows + tiles]
+
+    seconds = []
+    for peer in line_peers:
+        copy = pltpu.make_async_remote_copy(
+            src_ref=total, dst_ref=gather.at[me], send_sem=send2.at[peer],
+            recv_sem=recv2.at[me], device_id=(mine, peer), device_id_type=mesh_ids,
+        )
+        copy.start()
+        seconds.append(copy)
+    for peer in turn_peers:
+        copy = pltpu.make_async_remote_copy(
+            src_ref=root_total, dst_ref=root_box.at[mine], send_sem=send3.at[peer],
+            recv_sem=recv3.at[mine], device_id=(peer, me), device_id_type=mesh_ids,
+        )
+        copy.start()
+        seconds.append(copy)
+    gather[me] = total[...]
+    root_box[mine] = root_total[...]
+    for peer in line_peers:
+        pltpu.make_async_remote_copy(
+            src_ref=total, dst_ref=gather.at[peer], send_sem=send2.at[peer],
+            recv_sem=recv2.at[peer], device_id=(mine, peer), device_id_type=mesh_ids,
+        ).wait_recv()
+    for j, width in spans:
+        for d in range(line_size):
+            tree, line = divmod(d * rows, lines)
+            gain[tree, pl.ds(line, rows), pl.ds(j * LANE, LANE)] = gather[d, pl.ds(j * rows, rows), :]
+    for tree in range(trees):
+        regret = turn_ref[tree]
+        line_gain = gain[tree, :, :hands] / river_count
+        average = jnp.sum(regret_match(regret, 0) * line_gain, axis=0, keepdims=True)
+        out_ref[tree] = discount(regret) + line_gain - average
+    for peer in turn_peers:
+        pltpu.make_async_remote_copy(
+            src_ref=root_total, dst_ref=root_box.at[peer], send_sem=send3.at[peer],
+            recv_sem=recv3.at[peer], device_id=(peer, me), device_id_type=mesh_ids,
+        ).wait_recv()
+    value = root_box[0]
+    for d in range(1, turn_size):
+        value = value + root_box[d]
+    value = value / (river_count * tree_count)
+    for j, width in spans:
+        value_ref[:, pl.ds(j * LANE, width)] = value[j : j + 1, :width]
+    for copy in firsts + seconds:
+        copy.wait_send()
+
+
+def combine(node_sum, root, turn_regret, river_count, tree_count):
+    trees, lines, hands = node_sum.shape
+    line_size, turn_size = lax.axis_size("line"), lax.axis_size("turn")
+    tiles = -(-hands // LANE)
+    rows = trees * lines // line_size
+    up8 = lambda n: -(-n // 8) * 8
+    message, share, root_rows = up8(tiles * (rows + 1)), up8(tiles * rows), up8(tiles)
+    f32, dma = jnp.float32, pltpu.SemaphoreType.DMA
+    vmem = pl.BlockSpec(memory_space=pltpu.VMEM)
+    return pl.pallas_call(
+        functools.partial(combine_kernel, line_size, turn_size, river_count, tree_count),
+        out_shape=(
+            jax.ShapeDtypeStruct((trees, lines, hands), f32),
+            jax.ShapeDtypeStruct((1, hands), f32),
+        ),
+        in_specs=[vmem] * 3,
+        out_specs=(vmem, vmem),
+        scratch_shapes=[
+            pltpu.VMEM((line_size, message, LANE), f32),
+            pltpu.VMEM((line_size, message, LANE), f32),
+            pltpu.VMEM((share, LANE), f32),
+            pltpu.VMEM((line_size, share, LANE), f32),
+            pltpu.VMEM((root_rows, LANE), f32),
+            pltpu.VMEM((turn_size, root_rows, LANE), f32),
+            pltpu.VMEM((trees, lines, tiles * LANE), f32),
+            dma((line_size,)), dma((line_size,)),
+            dma((line_size,)), dma((line_size,)),
+            dma((turn_size,)), dma((turn_size,)),
+        ],
+        compiler_params=pltpu.CompilerParams(
+            collective_id=0, has_side_effects=True, vmem_limit_bytes=16 * 2**20
+        ),
+    )(node_sum, root, turn_regret)
 
 
 def body(turn_regret, river_regret, opp_reach, trav_reach, pot, blockers, ranks):
@@ -183,12 +318,8 @@
     new_river_regret, node_sum, root = run_local(
         turn_regret, river_regret, opp_reach, trav_reach, pot, blockers, ranks
     )
-    line_gain = lax.psum(node_sum, "line") / river_count
-    root_value = lax.psum(root[0], ("turn", "line")) / (tree_count * river_count)
-    turn_strategy = regret_match(turn_regret, 1)
-    node_turn = jnp.sum(turn_strategy * line_gain, axis=1)
-    new_turn_regret = discount(turn_regret) + line_gain - node_turn[:, None, :]
-    return (new_turn_regret, new_river_regret, root_value)
+    new_turn_regret, root_value = combine(node_sum, root, turn_regret, river_count, tree_count)
+    return (new_turn_regret, new_river_regret, root_value[0])
 
 
 def solution(mesh):

time: 117 us -> 42.6 us (0.36)
  blocking collectives: 42.1 us -> 0 us
  waiting for transfers between devices: 30 us -> 0 us
  Pallas kernels: 18.6 us -> 37.2 us
  between operations: 14.1 us -> 0.66 us
  local copies, waits for them, and re-layouts: 9.27 us -> 2.97 us
    psum x1 -> x0, blocking collectives: 42.1 us -> none  [body(): lax.psum(root[0], ('turn', 'line')) / (tree_count * river_count)]
    psum x1 -> x0, waiting for transfers between devices: 30 us -> none  [body(): line_gain = lax.psum(node_sum, 'line') / river_count]
    pallas_call x0 -> x1, Pallas kernels: none -> 17.6 us  [combine(): pl.pallas_call(functools.partial(combine_kernel, line_size, turn_size, ri...]
    unnamed x18 -> x7, local copies, waits for them, and re-layouts: 9.27 us -> 2.28 us
    sub x1 -> x0, other arithmetic: 1.81 us -> none  [body(): new_turn_regret = discount(turn_regret) + line_gain - node_turn[:, None, :]]
  transfers between devices with their start and end apart: 1 -> 0, of which waited for: 1 -> 0; matrix products, arithmetic and copies ran while one was open for 1% -> 0% of each run, Pallas kernels for 0% -> 0%
where the time goes in v2:
time: 42.6 us; the launch traced here: 42.4 us
  Pallas kernels  37.2 us (87%)
  local copies, waits for them, and re-layouts  2.97 us (7%)
  other arithmetic  1.62 us (4%)
  between operations  0.66 us (2%)
    pallas_call x1, Pallas kernels, run_local(): pl.pallas_call(functools.partial(runout_kernel, hands, rivers), grid=(tre...  19.6 us
    pallas_call x1, Pallas kernels, combine(): pl.pallas_call(functools.partial(combine_kernel, line_size, turn_size, ri...  17.6 us
    unnamed x7, local copies, waits for them, and re-layouts  2.28 us
    add x1, other arithmetic, run_local(): codes = jnp.pad(ranks * 2 + blockers, ((0, 0), (0, -rivers % 8), (0, 0)))  1 us

profile of v2, /device:TPU:0, one launch (start us, length us, event | category | flops | bytes accessed | tf_op | source)
XLA Modules:
  0.0 42.4 jit_solution(11306301056293350675)
XLA Ops:
  0.6 0.0 copy-start
  0.6 1.0 %copy_add_fusion = s32[4,3,1326]{2,1,0:T(4,128)S(1)} fusion(s32[4,3,1326]{2,0,1:T(4,128)} %param.13, s32[4,3,1326]{2,0,1:T(4,128)} %param.14), kind=kLoop, calls=%fused_computation | loop fusion | flops 31824 | bytes 190944 | tf_op jit(solution)/shard_map/add | solution.py:142
  1.6 0.7 %pad.4.code_ref = s32[4,8,1326]{2,1,0:T(8,128)} pad(s32[4,3,1326]{2,1,0:T(4,128)S(1)} %copy_add_fusion, s32[]{:T(128)} %constant.2.clone.1), padding=0_0x0_5x0_0 | pad | bytes 233380 | tf_op jit(solution)/shard_map/jit(_pad)/pad | solution.py:142
  2.3 19.6 %shard_map.103 = (f32[4,3,8,8,1326]{4,3,2,1,0:T(8,128)}, f32[4,8,1326]{2,1,0:T(8,128)}, f32[1,1326]{1,0:T(1,128)}) custom-call(f32[8,8]{1,0:T(8,128)} %pot_smem.1, bf16[1408,128]{1,0:T(8,128)(2,1)} %constant.6.clone.inc_ref, f32[4,3,8,8,1326]{4,3,2,1,0:T(8,128)} %regret_ref.1, f32[4,8,1326]{2,1,0:T(8,128)} %turn_ref.3, f32[4,1326]{1,0:T(4,128)} %opp_ref.1, ...), custom_call_target="tpu_custom_call" | custom-call | tf_op jit(solution)/shard_map/pallas_call | solution.py:146
  21.9 0.0 copy-done
  22.0 0.0 copy-start.1
  22.0 0.9 %copy-done.1 = f32[4,8,1326]{2,1,0:T(8,128)S(1)} copy-done((f32[4,8,1326]{2,1,0:T(8,128)S(1)}, f32[4,8,1326]{2,1,0:T(8,128)}, u32[]{:S(2)}) %copy-start.1) | copy-done | bytes 169752
  22.9 0.0 copy-start.2
  22.9 0.7 %copy-done.2 = f32[1,1326]{1,0:T(1,128)S(1)} copy-done((f32[1,1326]{1,0:T(1,128)S(1)}, f32[1,1326]{1,0:T(1,128)}, u32[]{:S(2)}) %copy-start.2) | copy-done | bytes 5328
  23.6 17.6 %shard_map.104 = (f32[4,8,1326]{2,1,0:T(8,128)S(1)}, f32[1,1326]{1,0:T(1,128)S(1)}) custom-call(f32[4,8,1326]{2,1,0:T(8,128)S(1)} %copy-done.1, f32[1,1326]{1,0:T(1,128)S(1)} %copy-done.2, f32[4,8,1326]{2,1,0:T(8,128)S(1)} %copy-done), custom_call_target="tpu_custom_call" | custom-call | tf_op jit(solution)/shard_map/pallas_call | solution.py:289
  41.1 0.6 %reduce = f32[1326]{0:T(1024)} reduce(f32[1,1326]{1,0:T(1,128)S(1)} %get-tuple-element.12, f32[]{:T(128)} %constant.12), dimensions={0}, to_apply=%get-tuple-element.12.reduce_sub_computation | reduce | bytes 10612 | tf_op jit(solution)/shard_map/pallas_call | solution.py:289
  41.8 0.7 %copy.21 = f32[4,8,1326]{2,1,0:T(8,128)} copy(f32[4,8,1326]{2,1,0:T(8,128)S(1)} %get-tuple-element.16) | data formatting | bytes 339456
Async XLA Ops:
  0.6 21.3 %copy-start = (f32[4,8,1326]{2,1,0:T(8,128)S(1)}, f32[4,8,1326]{2,1,0:T(8,128)}, u32[]{:S(2)}) copy-start(f32[4,8,1326]{2,1,0:T(8,128)} %turn_ref.3) | copy-start | bytes 509188
  22.0 0.9 %copy-start.1 = (f32[4,8,1326]{2,1,0:T(8,128)S(1)}, f32[4,8,1326]{2,1,0:T(8,128)}, u32[]{:S(2)}) copy-start(f32[4,8,1326]{2,1,0:T(8,128)} %get-tuple-element.8.node_ref) | copy-start | bytes 509188
  22.9 0.7 %copy-start.2 = (f32[1,1326]{1,0:T(1,128)S(1)}, f32[1,1326]{1,0:T(1,128)}, u32[]{:S(2)}) copy-start(f32[1,1326]{1,0:T(1,128)} %get-tuple-element.9.root_ref) | copy-start | bytes 15916

commit v3 on v2

--- a/solution.py
+++ b/solution.py
@@ -36,19 +36,43 @@
 
 
 def runout_kernel(
-    hands, rivers,
-    pot_smem, inc_ref, regret_ref, turn_ref, opp_ref, trav_ref, code_ref,
+    hands, rivers, steps,
+    pot_smem, inc_ref, regret_ref, next_ref, turn_ref, opp_ref, trav_ref, blk_ref, rank_ref,
     out_ref, node_ref, root_ref,
-    upper, lower, potb, stacked, phi, col, wgt, prod, root_acc,
+    upper, lower, potb, stacked, wgt, stacked_next, wgt_next, phi, col, root_acc,
 ):
-    tree, river = pl.program_id(0), pl.program_id(1)
+    step = pl.program_id(0)
+    tree, river = step // rivers, lax.rem(step, rivers)
     padded = upper.shape[0]
     lines = pot_smem.shape[0]
-    first = jnp.logical_and(tree == 0, river == 0)
-
-    @pl.when(first)
+    deep = 256
+
+    def rows_of(at_step):
+        at_tree = pl.ds(at_step // rivers, 1)
+        unblocked = blk_ref[lax.rem(at_step, rivers), at_tree, :].astype(jnp.float32)
+        return unblocked, opp_ref[at_tree, :]
+
+    def prepare(at_step, row_pair, source, start):
+        width = min(LANE, hands - start)
+        at = pl.ds(start, width)
+        at_tree = at_step // rivers
+        unblocked, opp = (row[:, start : start + width] for row in row_pair)
+        turn_strategy = regret_match(turn_ref[at_tree, :, at], 0)
+        opp_lines = (opp * turn_strategy).astype(jnp.bfloat16)
+        pos = jnp.maximum(source[0, :, :, at], 0.0)
+        total = jnp.sum(pos, axis=1)
+        potted = jnp.sum(pos * potb[:, :, :width], axis=1)
+        mean_pot = jnp.sum(potb[:, :, :width], axis=1) / lines
+        some = total > 0
+        weighted = jnp.where(some, potted / jnp.where(some, total, 1.0), mean_pot)
+        wgt_next[:, at] = weighted
+        trav = trav_ref[at_tree, :, at].astype(jnp.float32) * unblocked
+        both = jnp.concatenate([opp_lines.astype(jnp.float32) * unblocked * weighted, trav], axis=0)
+        stacked_next[:, at] = both.astype(jnp.bfloat16)
+
+    @pl.when(step == 0)
     def _():
-        stacked[...] = jnp.zeros_like(stacked)
+        stacked_next[...] = jnp.zeros_like(stacked_next)
         phi[...] = jnp.zeros_like(phi)
         root_acc[...] = jnp.zeros_like(root_acc)
         row = lax.broadcasted_iota(jnp.int32, (lines, LANE), 0)
@@ -66,130 +90,124 @@
             free = (1.0 - jnp.minimum(shared, 1.0)).astype(jnp.bfloat16)
             upper[rows, :] = free
             lower[rows, :] = -free
-
-    code = code_ref[0, pl.ds(river, 1), :]
-    unblocked = (code & 1).astype(jnp.float32)
-    rank = code >> 1
+        for start in range(0, hands, LANE):
+            prepare(0, rows_of(jnp.int32(0)), regret_ref, start)
+
+    stacked[...] = stacked_next[...]
+    wgt[...] = wgt_next[...]
+
+    @pl.when(river == 0)
+    def _():
+        node_ref[...] = jnp.zeros_like(node_ref)
+
+    rank = rank_ref[river, pl.ds(tree, 1), :]
     value = ((rank & 127) + 128).astype(jnp.float32)
     for bit in range(6):
         value = jnp.where((rank & (128 << bit)) != 0, value * float(2 ** (2**bit)), value)
     phi[:, :hands] = jnp.broadcast_to(value, (8, hands))
     col[...] = jnp.broadcast_to(phi[0:1, :], (LANE, padded)).T.astype(jnp.bfloat16)
 
-    turn_strategy = regret_match(turn_ref[0], 0)
-    opp_lines = (opp_ref[pl.ds(tree, 1), :] * turn_strategy).astype(jnp.bfloat16)
-    opp_part = opp_lines.astype(jnp.float32) * unblocked
-    trav = trav_ref[0].astype(jnp.float32)
-    for start in range(0, hands, LANE):
-        width = min(LANE, hands - start)
-        at = pl.ds(start, width)
-        pos = jnp.maximum(regret_ref[0, 0, :, :, at], 0.0)
-        total = jnp.sum(pos, axis=1)
-        potted = jnp.sum(pos * potb[:, :, :width], axis=1)
-        mean_pot = jnp.sum(potb[:, :, :width], axis=1) / lines
-        some = total > 0
-        wgt[:, at] = jnp.where(some, potted / jnp.where(some, total, 1.0), mean_pot)
-    weighted = wgt[:, :hands]
-    both = jnp.concatenate([opp_part * weighted, trav * unblocked], axis=0)
-    stacked[:, :hands] = both.astype(jnp.bfloat16)
-
-    row_phi = [jnp.broadcast_to(phi[:, pl.ds(j, LANE)], (8, LANE)).astype(jnp.bfloat16)[0:1] for j in range(0, padded, LANE)]
-    deep = 256
+    following = jnp.minimum(step + 1, steps - 1)
+    next_rows = rows_of(following)
+    scale = rows_of(step)[0] / hands
     for n0 in range(0, padded, deep):
         nw = min(deep, padded - n0)
+        row_phi = [phi[0:1, pl.ds(j, LANE)].astype(jnp.bfloat16) for j in range(n0, n0 + nw, LANE)]
         acc = jnp.zeros((2 * lines, nw), jnp.float32)
         for k0 in range(0, padded, deep):
-            kw = min(deep, padded - k0)
-            rows = pl.ds(k0, kw)
+            rows = pl.ds(k0, min(deep, padded - k0))
             parts = []
-            for j in range(n0, n0 + nw, LANE):
-                gap = row_phi[j // LANE] - col[rows, :]
-                cols = pl.ds(j, LANE)
+            for j in range(nw // LANE):
+                gap = row_phi[j] - col[rows, :]
+                cols = pl.ds(n0 + j * LANE, LANE)
                 parts.append(jnp.maximum(jnp.minimum(gap, upper[rows, cols]), lower[rows, cols]))
-            acc = acc + jnp.dot(stacked[:, rows], jnp.concatenate(parts, axis=1), preferred_element_type=jnp.float32)
-        prod[:, pl.ds(n0, nw)] = acc
-
-    scaled = unblocked / hands
-    root_acc[...] += trav * scaled * prod[:lines, :hands]
-    gain = scaled * prod[lines:, :hands]
-    node = gain * weighted
-
-    @pl.when(river == 0)
-    def _():
-        node_ref[0] = node
-
-    @pl.when(river > 0)
-    def _():
-        node_ref[0] += node
-
-    for l in range(lines):
-        for start in range(0, hands, LANE):
+            tile = jnp.concatenate(parts, axis=1)
+            acc = acc + jnp.dot(stacked[:, rows], tile, preferred_element_type=jnp.float32)
+        for start in range(n0, n0 + nw, LANE):
+            prepare(following, next_rows, next_ref, start)
             width = min(LANE, hands - start)
-            at = slice(start, start + width)
-            plane = discount(regret_ref[0, 0, l, :, at]) + potb[l, :, :width] * gain[l : l + 1, at]
-            out_ref[0, 0, l, :, at] = plane - node[l : l + 1, at]
-
-    @pl.when(jnp.logical_and(tree == pl.num_programs(0) - 1, river == rivers - 1))
+            at = pl.ds(start, width)
+            product = acc[:, start - n0 : start - n0 + width]
+            scaled = scale[:, start : start + width]
+            root_acc[:, at] += trav_ref[tree, :, at].astype(jnp.float32) * scaled * product[:lines]
+            gain = scaled * product[lines:]
+            node = gain * wgt[:, at]
+            node_ref[0, :, at] += node
+            for l in range(lines):
+                plane = discount(regret_ref[0, l, :, at]) + potb[l, :, :width] * gain[l : l + 1]
+                out_ref[0, l, :, at] = plane - node[l : l + 1]
+
+    @pl.when(step == steps - 1)
     def _():
         root_ref[...] = jnp.sum(root_acc[...], axis=0, keepdims=True)
 
 
 def run_local(turn_regret, river_regret, opp_reach, trav_reach, pot, blockers, ranks):
     trees, rivers, lines, _, hands = river_regret.shape
+    steps = trees * rivers
     padded = -(-hands // LANE) * LANE
-    table = incidence(hands, padded)
-    inc = jnp.asarray(table, jnp.bfloat16)
-    codes = jnp.pad(ranks * 2 + blockers, ((0, 0), (0, -rivers % 8), (0, 0)))
+    inc = jnp.asarray(incidence(hands, padded), jnp.bfloat16)
+    regrets = river_regret.reshape(steps, lines, lines, hands)
     bf, f32 = jnp.bfloat16, jnp.float32
-    per_tree = lambda s, r: (s, 0, 0)
-    whole = lambda s, r: (0, 0)
-    return pl.pallas_call(
-        functools.partial(runout_kernel, hands, rivers),
-        grid=(trees, rivers),
+    block = (1, lines, lines, hands)
+    outs = pl.pallas_call(
+        functools.partial(runout_kernel, hands, rivers, steps),
+        grid=(steps,),
         out_shape=(
-            jax.ShapeDtypeStruct(river_regret.shape, f32),
+            jax.ShapeDtypeStruct(regrets.shape, f32),
             jax.ShapeDtypeStruct((trees, lines, hands), f32),
             jax.ShapeDtypeStruct((1, hands), f32),
         ),
         in_specs=[
             pl.BlockSpec(memory_space=pltpu.SMEM),
-            pl.BlockSpec((padded, LANE), whole),
-            pl.BlockSpec((1, 1, lines, lines, hands), lambda s, r: (s, r, 0, 0, 0)),
-            pl.BlockSpec((1, lines, hands), per_tree),
-            pl.BlockSpec((trees, hands), whole),
-            pl.BlockSpec((1, lines, hands), per_tree),
-            pl.BlockSpec((1, codes.shape[1], hands), per_tree),
+            pl.BlockSpec((padded, LANE), lambda i: (0, 0)),
+            pl.BlockSpec(block, lambda i: (i, 0, 0, 0)),
+            pl.BlockSpec(block, lambda i: (jnp.minimum(i + 1, steps - 1), 0, 0, 0)),
+            pl.BlockSpec((trees, lines, hands), lambda i: (0, 0, 0)),
+            pl.BlockSpec((trees, hands), lambda i: (0, 0)),
+            pl.BlockSpec((trees, lines, hands), lambda i: (0, 0, 0)),
+            pl.BlockSpec((rivers, trees, hands), lambda i: (0, 0, 0)),
+            pl.BlockSpec((rivers, trees, hands), lambda i: (0, 0, 0)),
         ],
         out_specs=(
-            pl.BlockSpec((1, 1, lines, lines, hands), lambda s, r: (s, r, 0, 0, 0)),
-            pl.BlockSpec((1, lines, hands), per_tree),
-            pl.BlockSpec((1, hands), whole),
+            pl.BlockSpec(block, lambda i: (i, 0, 0, 0)),
+            pl.BlockSpec((1, lines, hands), lambda i: (i // rivers, 0, 0)),
+            pl.BlockSpec((1, hands), lambda i: (0, 0)),
         ),
         scratch_shapes=[
             pltpu.VMEM((padded, padded), bf),
             pltpu.VMEM((padded, padded), bf),
             pltpu.VMEM((lines, lines, LANE), f32),
             pltpu.VMEM((2 * lines, padded), bf),
+            pltpu.VMEM((lines, padded), f32),
+            pltpu.VMEM((2 * lines, padded), bf),
+            pltpu.VMEM((lines, padded), f32),
             pltpu.VMEM((8, padded), f32),
             pltpu.VMEM((padded, LANE), bf),
-            pltpu.VMEM((lines, padded), f32),
-            pltpu.VMEM((2 * lines, padded), f32),
             pltpu.VMEM((lines, hands), f32),
         ],
         compiler_params=pltpu.CompilerParams(vmem_limit_bytes=60 * 2**20),
-    )(pot, inc, river_regret, turn_regret, opp_reach, trav_reach, codes)
+    )(pot, inc, regrets, regrets, turn_regret, opp_reach, trav_reach,
+      blockers.transpose(1, 0, 2), ranks.transpose(1, 0, 2))
+    return (outs[0].reshape(river_regret.shape),) + tuple(outs[1:])
 
 
 def combine_kernel(
     line_size, turn_size, river_count, tree_count,
-    node_ref, root_ref, turn_ref, out_ref, value_ref,
-    outbox, inbox, total, gather, root_total, root_box, gain,
+    node_hbm, root_hbm, turn_ref, out_ref, value_ref,
+    node_ref, root_ref, in_sem, outbox, inbox, total, gather, root_total, root_box, gain,
     send1, recv1, send2, recv2, send3, recv3,
 ):
     me, mine = lax.axis_index("line"), lax.axis_index("turn")
     line_peers = [lax.rem(me + i, line_size) for i in range(1, line_size)]
     turn_peers = [lax.rem(mine + i, turn_size) for i in range(1, turn_size)]
     mesh_ids = pl.DeviceIdType.MESH
+    loads = [
+        pltpu.make_async_copy(node_hbm, node_ref, in_sem.at[0]),
+        pltpu.make_async_copy(root_hbm, root_ref, in_sem.at[1]),
+    ]
+    for load in loads:
+        load.start()
     barrier = pltpu.get_barrier_semaphore()
     for peer in line_peers:
         pl.semaphore_signal(barrier, inc=1, device_id=(mine, peer), device_id_type=mesh_ids)
@@ -202,6 +220,8 @@
     spans = [(j, min(LANE, hands - j * LANE)) for j in range(tiles)]
     outbox[...] = jnp.zeros_like(outbox)
     gain[...] = jnp.zeros_like(gain)
+    for load in loads:
+        load.wait()
     for j, width in spans:
         at = pl.ds(j * LANE, width)
         for d in range(line_size):
@@ -292,9 +312,12 @@
             jax.ShapeDtypeStruct((trees, lines, hands), f32),
             jax.ShapeDtypeStruct((1, hands), f32),
         ),
-        in_specs=[vmem] * 3,
+        in_specs=[pl.BlockSpec(memory_space=pl.ANY)] * 2 + [vmem],
         out_specs=(vmem, vmem),
         scratch_shapes=[
+            pltpu.VMEM((trees, lines, hands), f32),
+            pltpu.VMEM((1, hands), f32),
+            dma((2,)),
             pltpu.VMEM((line_size, message, LANE), f32),
             pltpu.VMEM((line_size, message, LANE), f32),
             pltpu.VMEM((share, LANE), f32),
@@ -307,7 +330,7 @@
             dma((turn_size,)), dma((turn_size,)),
         ],
         compiler_params=pltpu.CompilerParams(
-            collective_id=0, has_side_effects=True, vmem_limit_bytes=16 * 2**20
+            collective_id=0, has_side_effects=True, vmem_limit_bytes=60 * 2**20
         ),
     )(node_sum, root, turn_regret)
 

time: 42.6 us -> 42.4 us (level)
  Pallas kernels: 37.2 us -> 38.6 us
  local copies, waits for them, and re-layouts: 2.97 us -> 1.6 us
    pallas_call x1, Pallas kernels: 17.6 us -> 19.2 us  [combine(): pl.pallas_call(functools.partial(combine_kernel, line_size, turn_size, ri...]
    add x1 -> x0, other arithmetic: 1 us -> none  [run_local(): codes = jnp.pad(ranks * 2 + blockers, ((0, 0), (0, -rivers % 8), (0, 0)))]
    pallas_call x1, other arithmetic: 0.62 us -> 1.31 us  [combine(): pl.pallas_call(functools.partial(combine_kernel, line_size, turn_size, ri...]
    pad x1 -> x0, local copies, waits for them, and re-layouts: 0.69 us -> none  [run_local(): codes = jnp.pad(ranks * 2 + blockers, ((0, 0), (0, -rivers % 8), (0, 0)))]
    unnamed x7 -> x1, local copies, waits for them, and re-layouts: 2.28 us -> 1.6 us
where the time goes in v3:
time: 42.4 us; the launch traced here: 42.1 us
  Pallas kernels  38.6 us (91%)
  local copies, waits for them, and re-layouts  1.6 us (4%)
  other arithmetic  1.31 us (3%)
  between operations  0.64 us (2%)
    pallas_call x1, Pallas kernels, run_local(): pl.pallas_call(functools.partial(runout_kernel, hands, rivers, steps), gr...  19.4 us
    pallas_call x1, Pallas kernels, combine(): pl.pallas_call(functools.partial(combine_kernel, line_size, turn_size, ri...  19.2 us
    unnamed x1, local copies, waits for them, and re-layouts  1.6 us
    pallas_call x1, other arithmetic, combine(): pl.pallas_call(functools.partial(combine_kernel, line_size, turn_size, ri...  1.31 us

profile of v3, /device:TPU:0, one launch (start us, length us, event | category | flops | bytes accessed | tf_op | source)
XLA Modules:
  0.0 42.1 jit_solution(11280120631409542026)
XLA Ops:
  0.6 19.4 %shard_map.103 = (f32[12,8,8,1326]{3,2,1,0:T(8,128)}, f32[4,8,1326]{2,1,0:T(8,128)}, f32[1,1326]{1,0:T(1,128)}) custom-call(f32[8,8]{1,0:T(8,128)} %pot_smem.1, bf16[1408,128]{1,0:T(8,128)(2,1)} %constant.2.clone.inc_ref, f32[12,8,8,1326]{3,2,1,0:T(8,128)} %bitcast.4, f32[12,8,8,1326]{3,2,1,0:T(8,128)} %bitcast.5, f32[4,8,1326]{2,1,0:T(8,128)} %turn_ref.3, ...), custom_call_target="tpu_custom_call" | custom-call | tf_op jit(solution)/shard_map/pallas_call | solution.py:153
  20.0 19.2 %shard_map.104 = (f32[4,8,1326]{2,1,0:T(8,128)}, f32[1,1326]{1,0:T(1,128)}) custom-call(f32[4,8,1326]{2,1,0:T(8,128)} %get-tuple-element.8.node_hbm, f32[1,1326]{1,0:T(1,128)} %get-tuple-element.9.root_hbm, f32[4,8,1326]{2,1,0:T(8,128)} %turn_ref.3), custom_call_target="tpu_custom_call" | custom-call | tf_op jit(solution)/shard_map/pallas_call | solution.py:309
  39.2 1.3 %reduce = f32[1326]{0:T(1024)} reduce(f32[1,1326]{1,0:T(1,128)} %get-tuple-element.12, f32[]{:T(128)} %constant.6), dimensions={0}, to_apply=%get-tuple-element.12.reduce_sub_computation | reduce | bytes 10612 | tf_op jit(solution)/shard_map/pallas_call | solution.py:309
  40.5 1.6 %copy.12 = f32[4,8,1326]{2,1,0:T(8,128)} copy(f32[4,8,1326]{2,1,0:T(8,128)} %get-tuple-element.16) | data formatting | bytes 339456

commit v4 on v3

--- a/solution.py
+++ b/solution.py
@@ -194,20 +194,14 @@
 
 def combine_kernel(
     line_size, turn_size, river_count, tree_count,
-    node_hbm, root_hbm, turn_ref, out_ref, value_ref,
-    node_ref, root_ref, in_sem, outbox, inbox, total, gather, root_total, root_box, gain,
+    node_ref, root_ref, turn_ref, out_ref, value_ref,
+    outbox, inbox, total, gather, root_total, root_box, gain,
     send1, recv1, send2, recv2, send3, recv3,
 ):
     me, mine = lax.axis_index("line"), lax.axis_index("turn")
     line_peers = [lax.rem(me + i, line_size) for i in range(1, line_size)]
     turn_peers = [lax.rem(mine + i, turn_size) for i in range(1, turn_size)]
     mesh_ids = pl.DeviceIdType.MESH
-    loads = [
-        pltpu.make_async_copy(node_hbm, node_ref, in_sem.at[0]),
-        pltpu.make_async_copy(root_hbm, root_ref, in_sem.at[1]),
-    ]
-    for load in loads:
-        load.start()
     barrier = pltpu.get_barrier_semaphore()
     for peer in line_peers:
         pl.semaphore_signal(barrier, inc=1, device_id=(mine, peer), device_id_type=mesh_ids)
@@ -220,8 +214,6 @@
     spans = [(j, min(LANE, hands - j * LANE)) for j in range(tiles)]
     outbox[...] = jnp.zeros_like(outbox)
     gain[...] = jnp.zeros_like(gain)
-    for load in loads:
-        load.wait()
     for j, width in spans:
         at = pl.ds(j * LANE, width)
         for d in range(line_size):
@@ -312,12 +304,9 @@
             jax.ShapeDtypeStruct((trees, lines, hands), f32),
             jax.ShapeDtypeStruct((1, hands), f32),
         ),
-        in_specs=[pl.BlockSpec(memory_space=pl.ANY)] * 2 + [vmem],
+        in_specs=[vmem] * 3,
         out_specs=(vmem, vmem),
         scratch_shapes=[
-            pltpu.VMEM((trees, lines, hands), f32),
-            pltpu.VMEM((1, hands), f32),
-            dma((2,)),
             pltpu.VMEM((line_size, message, LANE), f32),
             pltpu.VMEM((line_size, message, LANE), f32),
             pltpu.VMEM((share, LANE), f32),
@@ -330,7 +319,7 @@
             dma((turn_size,)), dma((turn_size,)),
         ],
         compiler_params=pltpu.CompilerParams(
-            collective_id=0, has_side_effects=True, vmem_limit_bytes=60 * 2**20
+            collective_id=0, has_side_effects=True, vmem_limit_bytes=16 * 2**20
         ),
     )(node_sum, root, turn_regret)
 

time: 42.4 us -> 40.8 us (0.962)
  Pallas kernels: 38.6 us -> 37 us
  other arithmetic: 1.31 us -> 0.62 us
  local copies, waits for them, and re-layouts: 1.6 us -> 2.28 us
    pallas_call x1, Pallas kernels: 19.2 us -> 17.6 us  [combine(): pl.pallas_call(functools.partial(combine_kernel, line_size, turn_size, ri...]
    pallas_call x1, other arithmetic: 1.31 us -> 0.62 us  [combine(): pl.pallas_call(functools.partial(combine_kernel, line_size, turn_size, ri...]
    unnamed x1 -> x7, local copies, waits for them, and re-layouts: 1.6 us -> 2.28 us
where the time goes in v4:
time: 40.8 us; the launch traced here: 40.6 us
  Pallas kernels  37 us (91%)
  local copies, waits for them, and re-layouts  2.28 us (6%)
  between operations  0.66 us (2%)
  other arithmetic  0.62 us (2%)
    pallas_call x1, Pallas kernels, run_local(): pl.pallas_call(functools.partial(runout_kernel, hands, rivers, steps), gr...  19.4 us
    pallas_call x1, Pallas kernels, combine(): pl.pallas_call(functools.partial(combine_kernel, line_size, turn_size, ri...  17.6 us
    unnamed x7, local copies, waits for them, and re-layouts  2.28 us

profile of v4, /device:TPU:0, one launch (start us, length us, event | category | flops | bytes accessed | tf_op | source)
XLA Modules:
  0.0 40.6 jit_solution(12599109838468445176)
XLA Ops:
  0.6 0.0 copy-start
  0.6 19.4 %shard_map.103 = (f32[12,8,8,1326]{3,2,1,0:T(8,128)}, f32[4,8,1326]{2,1,0:T(8,128)}, f32[1,1326]{1,0:T(1,128)}) custom-call(f32[8,8]{1,0:T(8,128)} %pot_smem.1, bf16[1408,128]{1,0:T(8,128)(2,1)} %constant.2.clone.inc_ref, f32[12,8,8,1326]{3,2,1,0:T(8,128)} %bitcast.4, f32[12,8,8,1326]{3,2,1,0:T(8,128)} %bitcast.5, f32[4,8,1326]{2,1,0:T(8,128)} %turn_ref.3, ...), custom_call_target="tpu_custom_call" | custom-call | tf_op jit(solution)/shard_map/pallas_call | solution.py:153
  20.1 0.0 copy-done
  20.1 0.0 copy-start.1
  20.1 0.9 %copy-done.1 = f32[4,8,1326]{2,1,0:T(8,128)S(1)} copy-done((f32[4,8,1326]{2,1,0:T(8,128)S(1)}, f32[4,8,1326]{2,1,0:T(8,128)}, u32[]{:S(2)}) %copy-start.1) | copy-done | bytes 169752
  21.0 0.0 copy-start.2
  21.0 0.7 %copy-done.2 = f32[1,1326]{1,0:T(1,128)S(1)} copy-done((f32[1,1326]{1,0:T(1,128)S(1)}, f32[1,1326]{1,0:T(1,128)}, u32[]{:S(2)}) %copy-start.2) | copy-done | bytes 5328
  21.7 17.6 %shard_map.104 = (f32[4,8,1326]{2,1,0:T(8,128)S(1)}, f32[1,1326]{1,0:T(1,128)S(1)}) custom-call(f32[4,8,1326]{2,1,0:T(8,128)S(1)} %copy-done.1, f32[1,1326]{1,0:T(1,128)S(1)} %copy-done.2, f32[4,8,1326]{2,1,0:T(8,128)S(1)} %copy-done), custom_call_target="tpu_custom_call" | custom-call | tf_op jit(solution)/shard_map/pallas_call | solution.py:301
  39.3 0.6 %reduce = f32[1326]{0:T(1024)} reduce(f32[1,1326]{1,0:T(1,128)S(1)} %get-tuple-element.12, f32[]{:T(128)} %constant.6), dimensions={0}, to_apply=%get-tuple-element.12.reduce_sub_computation | reduce | bytes 10612 | tf_op jit(solution)/shard_map/pallas_call | solution.py:301
  39.9 0.7 %copy.12 = f32[4,8,1326]{2,1,0:T(8,128)} copy(f32[4,8,1326]{2,1,0:T(8,128)S(1)} %get-tuple-element.16) | data formatting | bytes 339456
Async XLA Ops:
  0.6 19.4 %copy-start = (f32[4,8,1326]{2,1,0:T(8,128)S(1)}, f32[4,8,1326]{2,1,0:T(8,128)}, u32[]{:S(2)}) copy-start(f32[4,8,1326]{2,1,0:T(8,128)} %turn_ref.3) | copy-start | bytes 509188
  20.1 0.9 %copy-start.1 = (f32[4,8,1326]{2,1,0:T(8,128)S(1)}, f32[4,8,1326]{2,1,0:T(8,128)}, u32[]{:S(2)}) copy-start(f32[4,8,1326]{2,1,0:T(8,128)} %get-tuple-element.8.node_ref) | copy-start | bytes 509188
  21.0 0.7 %copy-start.2 = (f32[1,1326]{1,0:T(1,128)S(1)}, f32[1,1326]{1,0:T(1,128)}, u32[]{:S(2)}) copy-start(f32[1,1326]{1,0:T(1,128)} %get-tuple-element.9.root_ref) | copy-start | bytes 15916

commit v5 on v4

--- a/solution.py
+++ b/solution.py
@@ -195,7 +195,7 @@
 def combine_kernel(
     line_size, turn_size, river_count, tree_count,
     node_ref, root_ref, turn_ref, out_ref, value_ref,
-    outbox, inbox, total, gather, root_total, root_box, gain,
+    outbox, inbox, total, gather, root_total, root_box, gain, strategy,
     send1, recv1, send2, recv2, send3, recv3,
 ):
     me, mine = lax.axis_index("line"), lax.axis_index("turn")
@@ -213,7 +213,6 @@
     tiles = -(-hands // LANE)
     spans = [(j, min(LANE, hands - j * LANE)) for j in range(tiles)]
     outbox[...] = jnp.zeros_like(outbox)
-    gain[...] = jnp.zeros_like(gain)
     for j, width in spans:
         at = pl.ds(j * LANE, width)
         for d in range(line_size):
@@ -231,6 +230,10 @@
         copy.start()
         firsts.append(copy)
     inbox[me] = outbox[me]
+    gain[...] = jnp.zeros_like(gain)
+    for tree in range(trees):
+        strategy[tree] = regret_match(turn_ref[tree], 0)
+        out_ref[tree] = discount(turn_ref[tree])
     for peer in line_peers:
         pltpu.make_async_remote_copy(
             src_ref=outbox.at[peer], dst_ref=inbox.at[peer], send_sem=send1.at[peer],
@@ -270,10 +273,9 @@
             tree, line = divmod(d * rows, lines)
             gain[tree, pl.ds(line, rows), pl.ds(j * LANE, LANE)] = gather[d, pl.ds(j * rows, rows), :]
     for tree in range(trees):
-        regret = turn_ref[tree]
         line_gain = gain[tree, :, :hands] / river_count
-        average = jnp.sum(regret_match(regret, 0) * line_gain, axis=0, keepdims=True)
-        out_ref[tree] = discount(regret) + line_gain - average
+        average = jnp.sum(strategy[tree] * line_gain, axis=0, keepdims=True)
+        out_ref[tree] = out_ref[tree] + line_gain - average
     for peer in turn_peers:
         pltpu.make_async_remote_copy(
             src_ref=root_total, dst_ref=root_box.at[peer], send_sem=send3.at[peer],
@@ -314,6 +316,7 @@
             pltpu.VMEM((root_rows, LANE), f32),
             pltpu.VMEM((turn_size, root_rows, LANE), f32),
             pltpu.VMEM((trees, lines, tiles * LANE), f32),
+            pltpu.VMEM((trees, lines, hands), f32),
             dma((line_size,)), dma((line_size,)),
             dma((line_size,)), dma((line_size,)),
             dma((turn_size,)), dma((turn_size,)),

time: 40.8 us -> 40.7 us (level)
  no operation moved by 1% of the time
where the time goes in v5:
time: 40.7 us; the launch traced here: 40.5 us
  Pallas kernels  36.9 us (91%)
  local copies, waits for them, and re-layouts  2.28 us (6%)
  between operations  0.66 us (2%)
  other arithmetic  0.62 us (2%)
    pallas_call x1, Pallas kernels, run_local(): pl.pallas_call(functools.partial(runout_kernel, hands, rivers, steps), gr...  19.4 us
    pallas_call x1, Pallas kernels, combine(): pl.pallas_call(functools.partial(combine_kernel, line_size, turn_size, ri...  17.5 us
    unnamed x7, local copies, waits for them, and re-layouts  2.28 us

profile of v5, /device:TPU:0, one launch (start us, length us, event | category | flops | bytes accessed | tf_op | source)
XLA Modules:
  0.0 40.5 jit_solution(4166566617824112455)
XLA Ops:
  0.6 0.0 copy-start
  0.6 19.4 %shard_map.103 = (f32[12,8,8,1326]{3,2,1,0:T(8,128)}, f32[4,8,1326]{2,1,0:T(8,128)}, f32[1,1326]{1,0:T(1,128)}) custom-call(f32[8,8]{1,0:T(8,128)} %pot_smem.1, bf16[1408,128]{1,0:T(8,128)(2,1)} %constant.2.clone.inc_ref, f32[12,8,8,1326]{3,2,1,0:T(8,128)} %bitcast.4, f32[12,8,8,1326]{3,2,1,0:T(8,128)} %bitcast.5, f32[4,8,1326]{2,1,0:T(8,128)} %turn_ref.3, ...), custom_call_target="tpu_custom_call" | custom-call | tf_op jit(solution)/shard_map/pallas_call | solution.py:153
  20.1 0.0 copy-done
  20.1 0.0 copy-start.1
  20.1 0.9 %copy-done.1 = f32[4,8,1326]{2,1,0:T(8,128)S(1)} copy-done((f32[4,8,1326]{2,1,0:T(8,128)S(1)}, f32[4,8,1326]{2,1,0:T(8,128)}, u32[]{:S(2)}) %copy-start.1) | copy-done | bytes 169752
  21.0 0.0 copy-start.2
  21.0 0.7 %copy-done.2 = f32[1,1326]{1,0:T(1,128)S(1)} copy-done((f32[1,1326]{1,0:T(1,128)S(1)}, f32[1,1326]{1,0:T(1,128)}, u32[]{:S(2)}) %copy-start.2) | copy-done | bytes 5328
  21.7 17.5 %shard_map.104 = (f32[4,8,1326]{2,1,0:T(8,128)S(1)}, f32[1,1326]{1,0:T(1,128)S(1)}) custom-call(f32[4,8,1326]{2,1,0:T(8,128)S(1)} %copy-done.1, f32[1,1326]{1,0:T(1,128)S(1)} %copy-done.2, f32[4,8,1326]{2,1,0:T(8,128)S(1)} %copy-done), custom_call_target="tpu_custom_call" | custom-call | tf_op jit(solution)/shard_map/pallas_call | solution.py:303
  39.2 0.6 %reduce = f32[1326]{0:T(1024)} reduce(f32[1,1326]{1,0:T(1,128)S(1)} %get-tuple-element.12, f32[]{:T(128)} %constant.6), dimensions={0}, to_apply=%get-tuple-element.12.reduce_sub_computation | reduce | bytes 10612 | tf_op jit(solution)/shard_map/pallas_call | solution.py:303
  39.8 0.7 %copy.12 = f32[4,8,1326]{2,1,0:T(8,128)} copy(f32[4,8,1326]{2,1,0:T(8,128)S(1)} %get-tuple-element.16) | data formatting | bytes 339456
Async XLA Ops:
  0.6 19.4 %copy-start = (f32[4,8,1326]{2,1,0:T(8,128)S(1)}, f32[4,8,1326]{2,1,0:T(8,128)}, u32[]{:S(2)}) copy-start(f32[4,8,1326]{2,1,0:T(8,128)} %turn_ref.3) | copy-start | bytes 509188
  20.1 0.9 %copy-start.1 = (f32[4,8,1326]{2,1,0:T(8,128)S(1)}, f32[4,8,1326]{2,1,0:T(8,128)}, u32[]{:S(2)}) copy-start(f32[4,8,1326]{2,1,0:T(8,128)} %get-tuple-element.8.node_ref) | copy-start | bytes 509188
  21.0 0.7 %copy-start.2 = (f32[1,1326]{1,0:T(1,128)S(1)}, f32[1,1326]{1,0:T(1,128)}, u32[]{:S(2)}) copy-start(f32[1,1326]{1,0:T(1,128)} %get-tuple-element.9.root_ref) | copy-start | bytes 15916
